TPU v7x, 512 devices: a whole 4x4x16 slice. The times are simulated.
512 devices in a mesh: row: 16 (over z_hi, y, core), col: 32 (over z_lo, x).
Axes of the slice: x: 4, y: 4, z: 16 (z_hi: 2, z_lo: 8; z = z_hi * 8 + z_lo), core: 2. Of those that a mesh axis runs over, the one named last changes fastest.
Arguments:
- gradient: bfloat16 [3584, 3584], P('row', 'col'), may hold values from -6 to 6
- moment: float32 [3584, 3584], P('row', 'col'), may hold values from -1.5 to 1.5
- second: float32 [3584, 3584], P('row', 'col'), may hold values from 0.001 to 0.3
- left_factor: float32 [3584, 3584], P('row', 'col'), may hold values from -6 to 6
- right_factor: float32 [3584, 3584], P('row', 'col'), may hold values from -6 to 6
- left_basis_t: bfloat16 [3584, 3584], P('row', 'col'), may hold values from -0.09375 to 0.09375
- right_basis: bfloat16 [3584, 3584], P('row', 'col'), may hold values from -0.09375 to 0.09375
Outputs:
- left_out: float32 [3584, 3584], P('row', 'col')
- right_out: float32 [3584, 3584], P('row', 'col')
- moment_out: float32 [3584, 3584], P('row', 'col')
- second_out: float32 [3584, 3584], P('row', 'col')
- update: bfloat16 [3584, 3584], P('row', 'col')
All inputs are finite; a program needn't handle non-finite values.
Results may differ from a plain program's by a relative error of at most 0.03.
Values may be sent and summed in bfloat16 or wider, within the bound.
A program may use at most 64 MiB of HBM per device.

v0:
```python
import jax
import jax.numpy as jnp
from jax import lax
from jax.sharding import PartitionSpec as P

beta_moment = 0.9
beta_second = 0.95
beta_factor = 0.95
epsilon = 1e-08


def from_root(value, axis, source):
    kept = jnp.where(lax.axis_index(axis) == source, value, 0).astype(value.dtype)
    return lax.psum(kept, axis)


def contract_first(left_side, right_side):
    return lax.dot_general(
        left_side, right_side, (((0,), (0,)), ((), ())), preferred_element_type=jnp.float32
    )


def contract_last(left_side, right_side):
    return lax.dot_general(
        left_side, right_side, (((1,), (1,)), ((), ())), preferred_element_type=jnp.float32
    )


def per_device(gradient, moment, second, left_factor, right_factor, left_basis_t, right_basis):
    row_block, col_block = gradient.shape
    block_ratio = row_block // col_block
    row_index = lax.axis_index("row")
    col_index = lax.axis_index("col")
    moment_out = beta_moment * moment + (1.0 - beta_moment) * gradient.astype(jnp.float32)
    moment_half = moment_out.astype(jnp.bfloat16)
    grad_rows, basis_rows = (
        lax.all_gather(gradient, "col", axis=1, tiled=True),
        lax.all_gather(left_basis_t, "col", axis=1, tiled=True),
    )
    stacked = jnp.concatenate([gradient, moment_half], axis=1)
    operand_cols = lax.all_gather(stacked, "row", axis=0, tiled=True)
    grad_cols = operand_cols[:, :col_block]
    offset = col_index * col_block % row_block
    owner_row = col_index * col_block // row_block
    partner = from_root(lax.dynamic_slice_in_dim(grad_rows, offset, col_block, 0), "row", owner_row)
    left_out = beta_factor * left_factor + (1.0 - beta_factor) * contract_last(grad_rows, partner)
    pieces = []
    for piece_index in range(block_ratio):
        owned_panel = from_root(grad_cols, "col", row_index * block_ratio + piece_index)
        pieces.append(contract_first(owned_panel, grad_cols))
    gram_right = jnp.concatenate(pieces, axis=0)
    right_out = beta_factor * right_factor + (1.0 - beta_factor) * gram_right
    inner_both = jnp.dot(basis_rows, operand_cols, preferred_element_type=jnp.float32).astype(
        jnp.bfloat16
    )
    inner_pair = jnp.stack([inner_both[:, :col_block], inner_both[:, col_block:]], axis=0)
    rotated_rows = lax.all_gather(inner_pair, "col", axis=2, tiled=True)
    right_cols = lax.all_gather(right_basis, "row", axis=0, tiled=True)
    rotated = jnp.einsum(
        "sbk,kc->sbc", rotated_rows, right_cols, preferred_element_type=jnp.float32
    )
    grad_rot = rotated[0]
    moment_rot = rotated[1]
    second_out = beta_second * second + (1.0 - beta_second) * grad_rot * grad_rot
    direction = (moment_rot / (jnp.sqrt(second_out) + epsilon)).astype(jnp.bfloat16)
    panel_piece = basis_rows
    back_left = lax.psum_scatter(
        contract_first(panel_piece, direction).astype(jnp.bfloat16),
        "row",
        scatter_dimension=0,
        tiled=True,
    )
    panel_piece = right_cols
    update_t = lax.psum_scatter(
        contract_last(panel_piece, back_left).astype(jnp.bfloat16),
        "col",
        scatter_dimension=0,
        tiled=True,
    ).astype(jnp.float32)
    update = update_t.T.astype(jnp.bfloat16)
    return (left_out, right_out, moment_out, second_out, update)


def solution(mesh):
    placed = (
        P("row", "col"),
        P("row", "col"),
        P("row", "col"),
        P("row", "col"),
        P("row", "col"),
        P("row", "col"),
        P("row", "col"),
    )
    return jax.shard_map(
        per_device,
        mesh=mesh,
        in_specs=placed,
        out_specs=(
            P("row", "col"),
            P("row", "col"),
            P("row", "col"),
            P("row", "col"),
            P("row", "col"),
        ),
        check_vma=False,
    )
```

profile of v0, /device:TPU:8, one launch (start us, length us, event | category | flops | bytes accessed | tf_op | source)
XLA Modules:
  0.0 1850.8 jit_solution(2128337485240679584)
XLA Ops:
  7.2 1.6 fusion.18
  8.8 1.6 pad_maximum_fusion
  10.5 1.5 copy.29
  12.1 92.5 %all-gather.7.cloned.1.call-done = bf16[3584,224]{1,0:T(8,128)(2,1)} async-done(((bf16[224,224]{1,0:T(8,128)(2,1)}), bf16[3584,224]{1,0:T(8,128)(2,1)}) %all-gather.7.cloned.1.call-update) | async-done | bytes 1605648 | tf_op jit(solution)/shard_map/all_gather | solution.py:41
  104.6 217.4 %all-gather.9.cloned.1.call-done = bf16[224,3584]{0,1:T(8,128)(2,1)} async-done(((bf16[224,112]{0,1:T(8,128)(2,1)}), bf16[224,3584]{0,1:T(8,128)(2,1)}) %all-gather.9.cloned.1.call-update) | async-done | bytes 1605648 | tf_op jit(solution)/shard_map/all_gather | solution.py:38
  322.0 2.8 fusion.2
  326.5 39.4 %all_gather.19 = bf16[3584,112]{1,0:T(8,128)(2,1)S(1)} all-gather(bf16[224,112]{1,0:T(8,128)(2,1)S(1)} %copy-done.10), channel_id=1, replica_groups=mesh['row'=16,'col'=32] {'row'}, dimensions={0}, use_global_device_ids=true | all-gather | bytes 852992 | tf_op jit(solution)/shard_map/all_gather | solution.py:58
  365.9 186.0 %all-gather.11.cloned.1.call-done = bf16[2,224,3584]{1,2,0:T(8,128)(2,1)} async-done(((bf16[2,224,112]{1,2,0:T(8,128)(2,1)}), bf16[2,224,3584]{1,2,0:T(8,128)(2,1)}) %all-gather.11.cloned.1.call-update) | async-done | bytes 3211280 | tf_op jit(solution)/shard_map/all_gather | solution.py:57
  551.9 2.7 fusion.5
  556.0 1.3 copy.40
  557.5 219.2 %all-gather.5.cloned.1.call-done = bf16[224,3584]{0,1:T(8,128)(2,1)} async-done(((bf16[224,112]{0,1:T(8,128)(2,1)}), bf16[224,3584]{0,1:T(8,128)(2,1)}) %all-gather.5.cloned.1.call-update) | async-done | bytes 1605648 | tf_op jit(solution)/shard_map/all_gather | solution.py:37
  776.6 2.8 dynamic-slice_select_fusion
  779.5 1.4 broadcast_select_fusion.1
  781.0 103.6 %reduce-scatter.7.cloned.1.call-done = bf16[224,112]{1,0:T(8,128)(2,1)} async-done(((bf16[3584,112]{1,0:T(8,128)(2,1)}), bf16[224,112]{1,0:T(8,128)(2,1)}) %reduce-scatter.7.cloned.1.call-update) | async-done | bytes 50192
  884.6 1.4 fusion
  886.0 2.3 copy.42
  888.5 0.8 copy-done.9
  889.3 235.4 %all-reduce.4.cloned.1.call-done = bf16[112,3584]{0,1:T(8,128)(2,1)} async-done(((bf16[112,3584]{0,1:T(8,128)(2,1)}), bf16[112,3584]{0,1:T(8,128)(2,1)}) %all-reduce.4.cloned.1.call-update) | async-done | bytes 802832 | tf_op jit(solution)/shard_map/psum | solution.py:14
  1124.8 1.6 fusion.4
  1127.1 472.0 %all-reduce.6.cloned.1.call-done = (bf16[3584,112]{1,0:T(8,128)(2,1)}, bf16[3584,112]{1,0:T(8,128)(2,1)}) async-done(((bf16[3584,112]{1,0:T(8,128)(2,1)}, bf16[3584,112]{1,0:T(8,128)(2,1)}), (bf16[3584,112]{1,0:T(8,128)(2,1)}, bf16[3584,112]{1,0:T(8,128)(2,1)})) %all-reduce.6.cloned.1.call-update) | async-done | bytes 1605648 | tf_op jit(solution)/shard_map/psum | solution.py:14
  1599.1 1.9 fusion.7
  1601.0 1.7 fusion.9
  1604.3 238.2 %reduce-scatter.9.cloned.1.call-done = bf16[112,224]{1,0:T(8,128)(2,1)} async-done(((bf16[3584,224]{1,0:T(8,128)(2,1)}), bf16[112,224]{1,0:T(8,128)(2,1)}) %reduce-scatter.9.cloned.1.call-update) | async-done | bytes 50192
  1842.4 1.5 copy.43
  (49 shorter events, 5.9 us)
Async XLA Ops:
  7.2 97.4 %all-gather.7.cloned.1.call-start = ((), (), s32[]{:S(2)}) async-start(), calls=%async_computation.4 | async-start | bytes 1949696 | tf_op jit(solution)/shard_map/all_gather | solution.py:41
  10.4 311.6 %all-gather.9.cloned.1.call-start = ((), (), s32[]{:S(2)}) async-start(), calls=%async_computation.5 | async-start | bytes 1892352 | tf_op jit(solution)/shard_map/all_gather | solution.py:38
  12.0 313.5 %copy-start.4 = (bf16[224,112]{1,0:T(8,128)(2,1)S(1)}, bf16[224,112]{1,0:T(8,128)(2,1)}, u32[]{:S(2)}) copy-start(bf16[224,112]{1,0:T(8,128)(2,1)} %param.7) | copy-start | bytes 150532
  12.0 314.3 %copy-start.7 = (f32[224,112]{1,0:T(8,128)S(1)}, f32[224,112]{1,0:T(8,128)}, u32[]{:S(2)}) copy-start(f32[224,112]{1,0:T(8,128)} %param.9) | copy-start | bytes 301060
  12.0 314.4 %copy-start.10 = (bf16[224,112]{1,0:T(8,128)(2,1)S(1)}, bf16[224,112]{1,0:T(8,128)(2,1)}, u32[]{:S(2)}) copy-start(bf16[224,112]{1,0:T(8,128)(2,1)} %param.13) | copy-start | bytes 150532
  12.1 539.9 %all-gather.11.cloned.1.call-start = ((), (), s32[]{:S(2)}) async-start(), calls=%async_computation.6 | async-start | bytes 3784704 | tf_op jit(solution)/shard_map/all_gather | solution.py:57
  325.5 451.1 %all-gather.5.cloned.1.call-start = ((), (), s32[]{:S(2)}) async-start(), calls=%async_computation.2 | async-start | bytes 1892352 | tf_op jit(solution)/shard_map/all_gather | solution.py:37
  326.3 558.3 %reduce-scatter.7.cloned.1.call-start = ((), (), s32[]{:S(2)}) async-start(), calls=%async_computation.7 | async-start | bytes 974848
  365.9 189.4 %copy-start.1 = (bf16[224,3584]{0,1:T(8,128)(2,1)S(1)}, bf16[224,3584]{0,1:T(8,128)(2,1)}, u32[]{:S(2)}) copy-start(bf16[224,3584]{0,1:T(8,128)(2,1)} %all-gather.9.cloned.1.call-done) | copy-start | bytes 4816900
  554.7 0.6 copy-start.2
  557.3 222.2 %copy-start.5 = (bf16[3584,224]{1,0:T(8,128)(2,1)S(1)}, bf16[3584,224]{1,0:T(8,128)(2,1)}, u32[]{:S(2)}) copy-start(bf16[3584,224]{1,0:T(8,128)(2,1)} %all-gather.7.cloned.1.call-done) | copy-start | bytes 4816900
  557.4 567.4 %all-reduce.4.cloned.1.call-start = ((), (), s32[]{:S(2)}) async-start(), calls=%async_computation.3 | async-start | bytes 1835008 | tf_op jit(solution)/shard_map/psum | solution.py:14
  779.5 819.6 %all-reduce.6.cloned.1.call-start = ((), (), s32[]{:S(2)}) async-start(), calls=%async_computation.9 | async-start | bytes 3670016 | tf_op jit(solution)/shard_map/psum | solution.py:14
  781.0 1061.5 %reduce-scatter.9.cloned.1.call-start = ((), (), s32[]{:S(2)}) async-start(), calls=%async_computation.8 | async-start | bytes 1892352
  886.0 2.3 copy-start.8
  888.3 0.9 copy-start.9
  888.3 236.4 %copy-start = (bf16[224,3584]{0,1:T(8,128)(2,1)S(1)}, bf16[224,3584]{0,1:T(8,128)(2,1)}, u32[]{:S(2)}) copy-start(bf16[224,3584]{0,1:T(8,128)(2,1)} %all-gather.5.cloned.1.call-done) | copy-start | bytes 4816900
  1126.4 474.6 %copy-start.6 = (bf16[3584,224]{1,0:T(8,128)(2,1)S(1)}, bf16[3584,224]{1,0:T(8,128)(2,1)}, u32[]{:S(2)}) copy-start(bf16[3584,224]{1,0:T(8,128)(2,1)} %all-gather.7.cloned.1.call-done) | copy-start | bytes 4816900
  1601.0 2.5 copy-start.3
Sparse Core Ops, SparseCore 0:
  11.9 92.6 all-gather.6
  107.2 214.7 all-gather.8
  325.6 226.2 all-gather.10
  554.4 222.1 all-gather.4
  781.1 103.4 reduce-scatter.6
  887.4 237.3 all-reduce.3
  1128.0 471.0 all-reduce.5
  1601.9 240.4 reduce-scatter.8
where the time goes:
time: 1850 us
  waiting for transfers between devices  1760 us (95%)
  blocking collectives  39.4 us (2%)
    psum x2, waiting for transfers between devices, from_root(): return lax.psum(kept, axis)  707 us
    unnamed x10, waiting for transfers between devices  342 us
    all_gather x1, waiting for transfers between devices, per_device(): lax.all_gather(gradient, 'col', axis=1, tiled=True)  219 us
    all_gather x1, waiting for transfers between devices, per_device(): lax.all_gather(left_basis_t, 'col', axis=1, tiled=True)  217 us
    all_gather x1, waiting for transfers between devices, per_device(): rotated_rows = lax.all_gather(inner_pair, 'col', axis=2, tiled=True)  186 us
    all_gather x1, waiting for transfers between devices, per_device(): operand_cols = lax.all_gather(stacked, 'row', axis=0, tiled=True)  92.5 us
    all_gather x1, blocking collectives, per_device(): right_cols = lax.all_gather(right_basis, 'row', axis=0, tiled=True)  39.4 us
  transfers between devices with their start and end apart: 8, of which 8 were waited for; matrix products, arithmetic and copies ran while one was open for 1% of the time, Pallas kernels for 0%

commit v1 on v0

v1 whole, which is shorter than its diff:
```python
import functools

import jax
import jax.numpy as jnp
from jax import lax
from jax.experimental import pallas as pl
from jax.experimental.pallas import tpu as pltpu
from jax.sharding import PartitionSpec as P

beta_moment = 0.9
beta_second = 0.95
beta_factor = 0.95
epsilon = 1e-08

MESH = pl.DeviceIdType.MESH
LANES = 128
BF16 = jnp.bfloat16
F32 = jnp.float32
DIMS = (2, 4, 2, 8, 4)


def run(*steps):
    live = list(steps)
    while live:
        for one in list(live):
            try:
                next(one)
            except StopIteration:
                live.remove(one)


def both(first, second):
    if first is None:
        return second
    if second is None:
        return first
    return jnp.logical_and(first, second)


def when(condition, action):
    if condition is None:
        action()
    else:
        pl.when(condition)(action)


def kernel(
    dims, g_ref, m_ref, sec_ref, lf_ref, rf_ref, l_ref, r_ref,
    lo_ref, ro_ref, mo_ref, so_ref, up_ref,
    gm, lb, rb, hb, bt, bt_core, bt_half, bt_full, bt_zs, bt_zr, bt_acc,
    gt, gt_core, gt_half, gt_full, gt_zs, gt_zr, gt_acc,
    ut, ut_half, ut_full, ut_zs, ut_zu, ut_zd, ut_acc, part, turn, facing,
    ssem, rsem,
):
    ZH, Y, CORE, ZL, X = dims
    R, C = ZH * Y * CORE, ZL * X
    rows, cols = g_ref.shape
    row, col = lax.axis_index("row"), lax.axis_index("col")
    core, y, zh = row % CORE, (row // CORE) % Y, row // (CORE * Y)
    x, z = col % X, col // X

    def at_row(zh_, y_, core_):
        return ((zh_ * Y + y_) * CORE + core_, col)

    def at_col(z_, x_):
        return (row, z_ * X + x_)

    y_up, y_dn, y_far = (y + 1) % Y, (y + Y - 1) % Y, (y + 2) % Y
    x_up, x_dn, x_far = (x + 1) % X, (x + X - 1) % X, (x + 2) % X
    to_y_up, to_y_dn = at_row(zh, y_up, core), at_row(zh, y_dn, core)
    to_zh, to_core = at_row(1 - zh, y, core), at_row(zh, y, 1 - core)
    to_x_up, to_x_dn = at_col(z, x_up), at_col(z, x_dn)
    to_z_up, to_z_dn = at_col(z + 1, x), at_col(z - 1, x)
    some = to_x_up if X > 1 else to_core if CORE > 1 else to_y_up

    counts = {"send": 0, "recv": 0}

    def sems(kind, number):
        first = counts[kind]
        counts[kind] += number
        return first

    pending = []

    def send(source, target, s, r, device, condition=None):
        copy = pltpu.make_async_remote_copy(
            src_ref=source, dst_ref=target, send_sem=ssem.at[s], recv_sem=rsem.at[r],
            device_id=device, device_id_type=MESH,
        )
        when(condition, copy.start)
        pending.append((condition, copy))

    def arrive(target, r, condition=None):
        copy = pltpu.make_async_remote_copy(
            src_ref=target, dst_ref=target, send_sem=ssem.at[0], recv_sem=rsem.at[r],
            device_id=some, device_id_type=MESH,
        )
        when(condition, copy.wait_recv)

    def gather_cols(buf):
        half = buf.shape[1] // 2
        low, high = pl.ds(0, half), pl.ds(half, half)
        sz, rz = sems("send", 2 * ZL), sems("recv", ZL)
        sx, rx = sems("send", 4 * ZL), sems("recv", 4 * ZL)

        def slot(z_, x_):
            return z_ * X + x_

        def items(t):
            if t == 0:
                return [(z, None, 0)]
            return [(z - t, z >= t, 1), (z + t, z + t < ZL, -1)]

        def turn_corner(t):
            if X == 1:
                return
            for zo, ok, _ in items(t):
                arrive(buf.at[slot(zo, x_dn)], rx + 4 * zo, ok)
                send(buf.at[slot(zo, x_dn), low], buf.at[slot(zo, x_dn), low],
                     sx + 4 * zo + 2, rx + 4 * zo + 2, to_x_up, ok)
                arrive(buf.at[slot(zo, x_up)], rx + 4 * zo + 1, ok)
                send(buf.at[slot(zo, x_up), high], buf.at[slot(zo, x_up), high],
                     sx + 4 * zo + 3, rx + 4 * zo + 3, to_x_dn, ok)

        for t in range(ZL):
            for zo, ok, way in items(t):
                here = buf.at[slot(zo, x)]
                if t > 0:
                    arrive(here, rz + zo, ok)
                if way >= 0 and t < ZL - 1:
                    send(here, here, sz + zo, rz + zo, to_z_up, both(ok, z < ZL - 1))
                if way <= 0 and t < ZL - 1:
                    send(here, here, sz + ZL + zo, rz + zo, to_z_dn, both(ok, z > 0))
                if X > 1:
                    send(here, here, sx + 4 * zo, rx + 4 * zo, to_x_up, ok)
                    send(here, here, sx + 4 * zo + 1, rx + 4 * zo + 1, to_x_dn, ok)
            yield
            if t > 0:
                turn_corner(t - 1)
                yield
        turn_corner(ZL - 1)
        yield
        if X > 1:
            for zo in range(ZL):
                arrive(buf.at[slot(zo, x_far), low], rx + 4 * zo + 2)
                arrive(buf.at[slot(zo, x_far), high], rx + 4 * zo + 3)
            yield

    def gather_rows(buf):
        half = buf.shape[3] // 2
        low, high = pl.ds(0, half), pl.ds(half, half)
        sz, rz = sems("send", 1), sems("recv", 1)
        sy, ry = sems("send", 4 * ZH), sems("recv", 4 * ZH)
        sc, rc = sems("send", ZH), sems("recv", ZH)
        levels = [zh, 1 - zh][:ZH]
        here = buf.at[core, zh, y]
        if ZH > 1:
            send(here, here, sz, rz, to_zh)
        for k, zi in enumerate(levels):
            mine = buf.at[core, zi, y]
            if k == 1:
                yield
                arrive(mine, rz)
            if Y > 1:
                send(mine, mine, sy + 4 * k, ry + 4 * k, to_y_up)
                send(mine, mine, sy + 4 * k + 1, ry + 4 * k + 1, to_y_dn)
            if k == 0:
                yield
        yield
        for k, zi in enumerate(levels):
            if Y > 1:
                arrive(buf.at[core, zi, y_dn], ry + 4 * k)
                send(buf.at[core, zi, y_dn, low], buf.at[core, zi, y_dn, low],
                     sy + 4 * k + 2, ry + 4 * k + 2, to_y_up)
                arrive(buf.at[core, zi, y_up], ry + 4 * k + 1)
                send(buf.at[core, zi, y_up, high], buf.at[core, zi, y_up, high],
                     sy + 4 * k + 3, ry + 4 * k + 3, to_y_dn)
                yield
        for k, zi in enumerate(levels):
            if Y > 1:
                arrive(buf.at[core, zi, y_far, low], ry + 4 * k + 2)
                arrive(buf.at[core, zi, y_far, high], ry + 4 * k + 3)
            if CORE > 1:
                send(buf.at[core, zi], buf.at[core, zi], sc + k, rc + k, to_core)
            yield
        if CORE > 1:
            for k, zi in enumerate(levels):
                arrive(buf.at[1 - core, zi], rc + k)
            yield

    def add(target, value):
        target[...] = (target[...].astype(F32) + value[...].astype(F32)).astype(BF16)

    def scatter_rows(buf, from_core, halves, full, zs, zr, acc):
        sc, rc = sems("send", ZH), sems("recv", ZH)
        sy, ry = sems("send", 4 * ZH), sems("recv", 4 * ZH)
        sz, rz = sems("send", 1), sems("recv", 1)
        levels = [1 - zh, zh][-ZH:]
        if CORE > 1:
            for k, zi in enumerate(levels):
                send(buf.at[1 - core, zi], from_core.at[zi], sc + k, rc + k, to_core)
        yield
        for k, zi in enumerate(levels):
            if CORE > 1:
                arrive(from_core.at[zi], rc + k)
                add(buf.at[core, zi], from_core.at[zi])
            if Y > 1:
                send(buf.at[core, zi, y_far, 0], halves.at[zi, 0], sy + 4 * k, ry + 4 * k, to_y_up)
                send(buf.at[core, zi, y_far, 1], halves.at[zi, 1], sy + 4 * k + 1, ry + 4 * k + 1, to_y_dn)
            yield
        for k, zi in enumerate(levels):
            if Y > 1:
                arrive(halves.at[zi, 0], ry + 4 * k)
                add(buf.at[core, zi, y_up, 0], halves.at[zi, 0])
                send(buf.at[core, zi, y_up], full.at[zi, 0], sy + 4 * k + 2, ry + 4 * k + 2, to_y_up)
                arrive(halves.at[zi, 1], ry + 4 * k + 1)
                add(buf.at[core, zi, y_dn, 1], halves.at[zi, 1])
                send(buf.at[core, zi, y_dn], full.at[zi, 1], sy + 4 * k + 3, ry + 4 * k + 3, to_y_dn)
                yield
        for k, zi in enumerate(levels):
            total = buf[core, zi, y].astype(F32)
            if Y > 1:
                arrive(full.at[zi, 0], ry + 4 * k + 2)
                arrive(full.at[zi, 1], ry + 4 * k + 3)
                total = total + full[zi, 0].astype(F32) + full[zi, 1].astype(F32)
            if ZH > 1 and k == 0:
                zs[...] = total.astype(BF16)
                send(zs, zr, sz, rz, to_zh)
            else:
                acc[...] = total
            yield
        if ZH > 1:
            arrive(zr, rz)
            acc[...] = acc[...] + zr[...].astype(F32)
            yield

    def scatter_cols(buf, halves, full, zs, zu, zd, acc):
        sx, rx = sems("send", 4 * ZL), sems("recv", 4 * ZL)
        sz, ru, rd = sems("send", ZL), sems("recv", ZL), sems("recv", ZL)
        order = []
        for k in range((ZL + 1) // 2):
            order += [ZL - 1 - k, k]
        order = order[:ZL]

        def along(d):
            total = buf[d, x].astype(F32)
            if X > 1:
                arrive(full.at[d, 0], rx + 4 * d + 2)
                arrive(full.at[d, 1], rx + 4 * d + 3)
                total = total + full[d, 0].astype(F32) + full[d, 1].astype(F32)
            acc[d] = total

            def more(source, r):
                arrive(source.at[d], r + d)
                acc[d] = acc[d] + source[d].astype(F32)

            when(both(z < d, z > 0), lambda: more(zu, ru))
            when(both(z > d, z < ZL - 1), lambda: more(zd, rd))

            def store():
                zs[d] = acc[d].astype(BF16)

            when(z != d, store)
            send(zs.at[d], zu.at[d], sz + d, ru + d, to_z_up, z < d)
            send(zs.at[d], zd.at[d], sz + d, rd + d, to_z_dn, z > d)

        if X > 1:
            for d in order:
                send(buf.at[d, x_far, 0], halves.at[d, 0], sx + 4 * d, rx + 4 * d, to_x_up)
                send(buf.at[d, x_far, 1], halves.at[d, 1], sx + 4 * d + 1, rx + 4 * d + 1, to_x_dn)
        yield
        lag = min(3, ZL - 1)
        for k in range(ZL + lag):
            if k < ZL and X > 1:
                d = order[k]
                arrive(halves.at[d, 0], rx + 4 * d)
                add(buf.at[d, x_up, 0], halves.at[d, 0])
                send(buf.at[d, x_up], full.at[d, 0], sx + 4 * d + 2, rx + 4 * d + 2, to_x_up)
                arrive(halves.at[d, 1], rx + 4 * d + 1)
                add(buf.at[d, x_dn, 1], halves.at[d, 1])
                send(buf.at[d, x_dn], full.at[d, 1], sx + 4 * d + 3, rx + 4 * d + 3, to_x_dn)
                yield
            if k >= lag:
                along(order[k - lag])
                yield

        def more(source, r):
            arrive(source.at[z], r + z)
            acc[z] = acc[z] + source[z].astype(F32)

        when(z > 0, lambda: more(zu, ru))
        when(z < ZL - 1, lambda: more(zd, rd))
        yield

    def broadcast_partner():
        owner = col // 2
        core0, y0, zh0 = owner % CORE, (owner // CORE) % Y, owner // (CORE * Y)
        away = (y + Y - y0) % Y
        same_core, same_zh = core == core0, zh == zh0
        chunks = 4
        size = C // chunks
        sz, rz = sems("send", chunks), sems("recv", chunks)
        sy, ry = sems("send", 4 * chunks), sems("recv", 4 * chunks)
        sc, rc = sems("send", chunks), sems("recv", chunks)

        for parity in range(2):
            @pl.when(both(row == owner, col % 2 == parity))
            def _():
                part[...] = gm[:, parity * cols:(parity + 1) * cols, :]

        yield
        source = both(same_core, away == 0)
        for n in range(chunks):
            piece = part.at[pl.ds(n * size, size)]
            if ZH > 1:
                send(piece, piece, sz + n, rz + n, to_zh, both(source, same_zh))
        for n in range(chunks):
            first = part.at[pl.ds(n * size, size // 2)]
            second = part.at[pl.ds(n * size + size // 2, size // 2)]
            piece = part.at[pl.ds(n * size, size)]
            if ZH > 1:
                arrive(piece, rz + n, both(source, jnp.logical_not(same_zh)))
            if Y > 1:
                send(piece, piece, sy + 4 * n, ry + 4 * n, to_y_up, source)
                send(piece, piece, sy + 4 * n + 1, ry + 4 * n + 1, to_y_dn, source)
                yield
                one, three = both(same_core, away == 1), both(same_core, away == 3)
                arrive(piece, ry + 4 * n, one)
                send(first, first, sy + 4 * n + 2, ry + 4 * n + 2, to_y_up, one)
                arrive(piece, ry + 4 * n + 1, three)
                send(second, second, sy + 4 * n + 3, ry + 4 * n + 3, to_y_dn, three)
                yield
                two = both(same_core, away == 2)
                arrive(first, ry + 4 * n + 2, two)
                arrive(second, ry + 4 * n + 3, two)
            if CORE > 1:
                send(piece, piece, sc + n, rc + n, to_core, same_core)
            yield
        if CORE > 1:
            for n in range(chunks):
                piece = part.at[pl.ds(n * size, size)]
                arrive(piece, rc + n, jnp.logical_not(same_core))
            yield

    def place(p):
        return p % CORE, p // (CORE * Y), (p // CORE) % Y

    def spread(block):
        pad = jnp.zeros((LANES - cols, block.shape[1]), block.dtype)
        return jnp.concatenate([block[:cols], pad, block[cols:], pad], axis=0)

    def pair(buf, p, top=0):
        return jnp.concatenate(
            [buf[2 * p, top:top + rows], buf[2 * p + 1, top:top + rows]], axis=1
        )

    def left_terms(side, buf, target):
        turned = side.astype(F32).T.astype(BF16)
        for p in range(R):
            term = jnp.dot(turned, pair(buf, p), preferred_element_type=F32)[:cols].astype(BF16)
            c, h, j = place(p)
            target[c, h, j, 0] = term[:, :LANES]
            target[c, h, j, 1] = term[:, LANES:]

    def turned_block(acc, h):
        turn[0:cols, :] = acc
        return turn[...].T[:cols, :cols]

    g = g_ref[...]
    moment = beta_moment * m_ref[...] + (1.0 - beta_moment) * g.astype(F32)
    mo_ref[...] = moment
    gm[col] = jnp.zeros(gm.shape[1:], BF16)
    lb[col] = jnp.zeros(lb.shape[1:], BF16)
    rb[core, zh, y] = jnp.zeros(rb.shape[3:], BF16)
    gm[col, 0:rows, 0:cols] = g
    gm[col, rows:2 * rows, 0:cols] = moment.astype(BF16)
    lb[col, :, 0:cols] = l_ref[...]
    rb[core, zh, y, :, 0:cols] = r_ref[...]
    turn[...] = jnp.zeros(turn.shape, F32)

    barrier = pltpu.get_barrier_semaphore()

    def greet(device):
        pl.semaphore_signal(barrier, inc=1, device_id=device, device_id_type=MESH)

    always = 0
    for present, devices in (
        (ZH > 1, (to_zh,)), (CORE > 1, (to_core,)), (Y > 1, (to_y_up, to_y_dn)), (X > 1, (to_x_up, to_x_dn)),
    ):
        if present:
            for device in devices:
                greet(device)
                always += 1
    if ZL > 1:
        pl.when(z < ZL - 1)(lambda: greet(to_z_up))
        pl.when(z > 0)(lambda: greet(to_z_dn))
        inner = both(z > 0, z < ZL - 1)
        pl.when(inner)(lambda: pl.semaphore_wait(barrier, always + 2))
        pl.when(jnp.logical_not(inner))(lambda: pl.semaphore_wait(barrier, always + 1))
    else:
        pl.semaphore_wait(barrier, always)

    run(gather_cols(gm), gather_rows(rb))
    rotated = jnp.zeros((2 * rows, LANES), F32)
    for p in range(R):
        both_blocks = jnp.concatenate([gm[2 * p], gm[2 * p + 1]], axis=1)
        rotated = rotated + jnp.dot(both_blocks, spread(rb[place(p)]), preferred_element_type=F32)
    hb[core, zh, y, :, 0:LANES] = rotated[:rows].astype(BF16)
    hb[core, zh, y, :, LANES:2 * LANES] = rotated[rows:].astype(BF16)

    def right_factor_terms():
        left_terms(gm[col, 0:rows, :], gm, gt)
        yield

    run(gather_rows(hb), gather_cols(lb), right_factor_terms())
    rot = jnp.zeros((rows, 2 * LANES), F32)
    for p in range(R):
        rot = rot + jnp.dot(pair(lb, p), spread(hb[place(p)]), preferred_element_type=F32)
    grad_rot, moment_rot = rot[:, 0:cols], rot[:, LANES:LANES + cols]
    second = beta_second * sec_ref[...] + (1.0 - beta_second) * grad_rot * grad_rot
    so_ref[...] = second
    direction = moment_rot / (jnp.sqrt(second) + epsilon)
    facing[...] = jnp.zeros(facing.shape, BF16)
    facing[:, 0:cols] = direction.astype(BF16)

    left_terms(facing[...], lb, bt)
    run(scatter_rows(bt, bt_core, bt_half, bt_full, bt_zs, bt_zr, bt_acc))
    back = jnp.concatenate([bt_acc[0], bt_acc[1]], axis=1).astype(BF16)
    back = jnp.concatenate([back, jnp.zeros((LANES - cols, 2 * LANES), BF16)], axis=0)

    for p in range(R):
        term = jnp.dot(rb[place(p)], back, preferred_element_type=F32).astype(BF16)
        for k in range(2):
            c = 2 * p + k
            for h in range(2):
                ut[c // X, c % X, h] = term[k * cols:(k + 1) * cols, h * LANES:(h + 1) * LANES]
    run(
        scatter_cols(ut, ut_half, ut_full, ut_zs, ut_zu, ut_zd, ut_acc),
        scatter_rows(gt, gt_core, gt_half, gt_full, gt_zs, gt_zr, gt_acc),
        broadcast_partner(),
    )
    left = jnp.zeros((rows, cols), F32)
    for p in range(R):
        left = left + lax.dot_general(
            pair(gm, p), jnp.concatenate([part[2 * p], part[2 * p + 1]], axis=1),
            (((1,), (1,)), ((), ())), preferred_element_type=F32,
        )
    lo_ref[...] = beta_factor * lf_ref[...] + (1.0 - beta_factor) * left
    for h in range(2):
        part_rows = pl.ds(h * cols, cols)
        ro_ref[part_rows, :] = beta_factor * rf_ref[part_rows, :] + (1.0 - beta_factor) * turned_block(gt_acc[h], h)
        up_ref[part_rows, :] = turned_block(ut_acc[z, h], h).astype(BF16)

    for condition, copy in pending:
        when(condition, copy.wait_send)


def per_device(dims, gradient, moment, second, left_factor, right_factor, left_basis_t, right_basis):
    ZH, Y, CORE, ZL, X = dims
    rows, cols = gradient.shape
    C = ZL * X

    def half_blocks(*lead, dtype=BF16):
        return pltpu.VMEM((*lead, 2, cols, LANES), dtype)

    def row_sum():
        return [
            half_blocks(CORE, ZH, Y), half_blocks(ZH, Y), pltpu.VMEM((ZH, 2, cols, LANES), BF16),
            half_blocks(ZH, 2), half_blocks(), half_blocks(), half_blocks(dtype=F32),
        ]

    block = jax.ShapeDtypeStruct((rows, cols), F32)
    return pl.pallas_call(
        functools.partial(kernel, dims),
        out_shape=(block, block, block, block, jax.ShapeDtypeStruct((rows, cols), BF16)),
        in_specs=[pl.BlockSpec(memory_space=pltpu.VMEM)] * 7,
        out_specs=[pl.BlockSpec(memory_space=pltpu.VMEM)] * 5,
        scratch_shapes=[
            pltpu.VMEM((C, 2 * rows, LANES), BF16),
            pltpu.VMEM((C, rows, LANES), BF16),
            pltpu.VMEM((CORE, ZH, Y, rows, LANES), BF16),
            pltpu.VMEM((CORE, ZH, Y, rows, 2 * LANES), BF16),
            *row_sum(),
            *row_sum(),
            half_blocks(ZL, X), pltpu.VMEM((ZL, 2, cols, LANES), BF16), half_blocks(ZL, 2),
            half_blocks(ZL), half_blocks(ZL), half_blocks(ZL), half_blocks(ZL, dtype=F32),
            pltpu.VMEM((C, cols, LANES), BF16),
            pltpu.VMEM((LANES, LANES), F32),
            pltpu.VMEM((rows, LANES), BF16),
            pltpu.SemaphoreType.DMA((256,)),
            pltpu.SemaphoreType.DMA((256,)),
        ],
        compiler_params=pltpu.CompilerParams(
            collective_id=0, has_side_effects=True, vmem_limit_bytes=48 << 20
        ),
    )(gradient, moment, second, left_factor, right_factor, left_basis_t, right_basis)


def build(mesh, dims):
    placed = P("row", "col")
    return jax.shard_map(
        functools.partial(per_device, dims),
        mesh=mesh,
        in_specs=(placed,) * 7,
        out_specs=(placed,) * 5,
        check_vma=False,
    )


def solution(mesh):
    return build(mesh, DIMS)
```

time: 1850 us -> 225 us (0.12)
  the two profiles are of different devices: /device:TPU:8 before, /device:TPU:384 now
where the time goes in v1:
time: 225 us
  Pallas kernels  215 us (96%)
  local copies, waits for them, and re-layouts  9.25 us (4%)
    pallas_call x1, Pallas kernels, per_device(): pl.pallas_call(functools.partial(kernel, dims), out_shape=(block, block,...  215 us
    unnamed x19, local copies, waits for them, and re-layouts  9.25 us

profile of v1, /device:TPU:384, one launch (start us, length us, event | category | flops | bytes accessed | tf_op | source)
XLA Modules:
  0.0 225.1 jit_solution(11734872406537252119)
XLA Ops:
  0.6 0.0 copy-start
  0.6 0.9 copy-done
  1.5 0.0 copy-start.1
  1.5 0.9 copy-done.1
  2.4 0.0 copy-start.2
  2.4 0.9 copy-done.2
  3.3 0.0 copy-start.3
  3.3 0.9 copy-done.3
  4.2 0.0 copy-start.4
  4.2 0.8 copy-done.4
  5.0 0.0 copy-start.5
  5.1 0.8 copy-done.5
  5.9 0.0 copy-start.6
  5.9 0.8 copy-done.6
  6.7 215.2 %shard_map.110 = (f32[224,112]{1,0:T(8,128)S(1)}, f32[224,112]{1,0:T(8,128)S(1)}, f32[224,112]{1,0:T(8,128)S(1)}, f32[224,112]{1,0:T(8,128)S(1)}, bf16[224,112]{1,0:T(8,128)(2,1)S(1)}) custom-call(bf16[224,112]{1,0:T(8,128)(2,1)S(1)} %copy-done.4, f32[224,112]{1,0:T(8,128)S(1)} %copy-done, f32[224,112]{1,0:T(8,128)S(1)} %copy-done.1, ...), custom_call_target="tpu_custom_call" | custom-call | tf_op jit(solution)/shard_map/pallas_call | solution.py:473
  221.9 0.6 copy.17
  222.5 0.6 copy.18
  223.2 0.6 copy.19
  223.8 0.6 copy.20
  224.5 0.6 copy.21
Async XLA Ops:
  0.6 0.9 copy-start
  1.5 0.9 copy-start.1
  2.4 0.9 copy-start.2
  3.3 0.9 copy-start.3
  4.2 0.8 copy-start.4
  5.0 0.8 copy-start.5
  5.9 0.8 copy-start.6

commit v2 on v1

--- a/solution.py
+++ b/solution.py
@@ -17,6 +17,9 @@
 BF16 = jnp.bfloat16
 F32 = jnp.float32
 DIMS = (2, 4, 2, 8, 4)
+LAG = 1
+MOMENT_LATER = 0
+BASIS_LATER = 0
 
 
 def run(*steps):
@@ -45,12 +48,13 @@
 
 
 def kernel(
-    dims, g_ref, m_ref, sec_ref, lf_ref, rf_ref, l_ref, r_ref,
+    dims, g_hbm, m_hbm, sec_hbm, lf_hbm, rf_hbm, l_hbm, r_hbm,
     lo_ref, ro_ref, mo_ref, so_ref, up_ref,
-    gm, lb, rb, hb, bt, bt_core, bt_half, bt_full, bt_zs, bt_zr, bt_acc,
+    g_ref, m_ref, sec_ref, lf_ref, rf_ref, l_ref, r_ref,
+    gb, mb, lb, rb, hg, hm, bt, bt_core, bt_half, bt_full, bt_zs, bt_zr, bt_acc,
     gt, gt_core, gt_half, gt_full, gt_zs, gt_zr, gt_acc,
-    ut, ut_half, ut_full, ut_zs, ut_zu, ut_zd, ut_acc, part, turn, facing,
-    ssem, rsem,
+    ut, ut_half, ut_full, ut_zs, ut_za, ut_zb, ut_zt, ut_zc, ut_other, ut_acc, part, turn, facing,
+    ssem, rsem, lsem,
 ):
     ZH, Y, CORE, ZL, X = dims
     R, C = ZH * Y * CORE, ZL * X
@@ -58,6 +62,8 @@
     row, col = lax.axis_index("row"), lax.axis_index("col")
     core, y, zh = row % CORE, (row // CORE) % Y, row // (CORE * Y)
     x, z = col % X, col // X
+    H = ZL // 2
+    i, ours, there = z % H, z // H * H, (1 - z // H) * H
 
     def at_row(zh_, y_, core_):
         return ((zh_ * Y + y_) * CORE + core_, col)
@@ -70,6 +76,10 @@
     to_y_up, to_y_dn = at_row(zh, y_up, core), at_row(zh, y_dn, core)
     to_zh, to_core = at_row(1 - zh, y, core), at_row(zh, y, 1 - core)
     to_x_up, to_x_dn = at_col(z, x_up), at_col(z, x_dn)
+    mirror = [(col // 2, 2 * row + e) for e in range(2)]
+    mirror_core = (col // 2) % CORE
+    mirror_y_zh = ((col // 2 // CORE) % Y, col // 2 // (CORE * Y))
+    itself = [both(row == col // 2, col % 2 == e) for e in range(2)]
     to_z_up, to_z_dn = at_col(z + 1, x), at_col(z - 1, x)
     some = to_x_up if X > 1 else to_core if CORE > 1 else to_y_up
 
@@ -135,11 +145,12 @@
                     send(here, here, sx + 4 * zo, rx + 4 * zo, to_x_up, ok)
                     send(here, here, sx + 4 * zo + 1, rx + 4 * zo + 1, to_x_dn, ok)
             yield
-            if t > 0:
-                turn_corner(t - 1)
-                yield
-        turn_corner(ZL - 1)
-        yield
+            if t >= LAG:
+                turn_corner(t - LAG)
+                yield
+        for t in range(ZL - LAG, ZL):
+            turn_corner(t)
+            yield
         if X > 1:
             for zo in range(ZL):
                 arrive(buf.at[slot(zo, x_far), low], rx + 4 * zo + 2)
@@ -234,113 +245,77 @@
             acc[...] = acc[...] + zr[...].astype(F32)
             yield
 
-    def scatter_cols(buf, halves, full, zs, zu, zd, acc):
+    def scatter_cols(buf, halves, full, zs, za, zb, zt, zc, other, acc):
         sx, rx = sems("send", 4 * ZL), sems("recv", 4 * ZL)
-        sz, ru, rd = sems("send", ZL), sems("recv", ZL), sems("recv", ZL)
-        order = []
-        for k in range((ZL + 1) // 2):
-            order += [ZL - 1 - k, k]
-        order = order[:ZL]
-
-        def along(d):
+        sz, ra, rb_ = sems("send", ZL), sems("recv", H), sems("recv", H)
+        sc, rc = sems("send", 1), sems("recv", 1)
+        order = [there + j for j in range(H)] + [ours + j for j in range(H)]
+        if X > 1:
+            for k, d in enumerate(order):
+                send(buf.at[d, x_far, 0], halves.at[k, 0], sx + 4 * k, rx + 4 * k, to_x_up)
+                send(buf.at[d, x_far, 1], halves.at[k, 1], sx + 4 * k + 1, rx + 4 * k + 1, to_x_dn)
+        yield
+
+        def along(k):
+            d, j = order[k], k % H
             total = buf[d, x].astype(F32)
             if X > 1:
-                arrive(full.at[d, 0], rx + 4 * d + 2)
-                arrive(full.at[d, 1], rx + 4 * d + 3)
-                total = total + full[d, 0].astype(F32) + full[d, 1].astype(F32)
-            acc[d] = total
-
-            def more(source, r):
-                arrive(source.at[d], r + d)
-                acc[d] = acc[d] + source[d].astype(F32)
-
-            when(both(z < d, z > 0), lambda: more(zu, ru))
-            when(both(z > d, z < ZL - 1), lambda: more(zd, rd))
-
-            def store():
-                zs[d] = acc[d].astype(BF16)
-
-            when(z != d, store)
-            send(zs.at[d], zu.at[d], sz + d, ru + d, to_z_up, z < d)
-            send(zs.at[d], zd.at[d], sz + d, rd + d, to_z_dn, z > d)
-
-        if X > 1:
-            for d in order:
-                send(buf.at[d, x_far, 0], halves.at[d, 0], sx + 4 * d, rx + 4 * d, to_x_up)
-                send(buf.at[d, x_far, 1], halves.at[d, 1], sx + 4 * d + 1, rx + 4 * d + 1, to_x_dn)
-        yield
-        lag = min(3, ZL - 1)
+                arrive(full.at[k, 0], rx + 4 * k + 2)
+                arrive(full.at[k, 1], rx + 4 * k + 3)
+                total = total + full[k, 0].astype(F32) + full[k, 1].astype(F32)
+            zs[k] = total.astype(BF16)
+            target, keep, r = (za, other, ra) if k < H else (zb, acc, rb_)
+            send(zs.at[k], target.at[i], sz + k, r + i, at_col(ours + j, x), i != j)
+
+            @pl.when(i == j)
+            def _():
+                keep[...] = total
+
+        def gathered(source, r, into):
+            for j in range(H):
+                @pl.when(i != j)
+                def _():
+                    arrive(source.at[j], r + j)
+                    into[...] = into[...] + source[j].astype(F32)
+
+        lag = min(2, ZL - 1)
         for k in range(ZL + lag):
             if k < ZL and X > 1:
                 d = order[k]
-                arrive(halves.at[d, 0], rx + 4 * d)
-                add(buf.at[d, x_up, 0], halves.at[d, 0])
-                send(buf.at[d, x_up], full.at[d, 0], sx + 4 * d + 2, rx + 4 * d + 2, to_x_up)
-                arrive(halves.at[d, 1], rx + 4 * d + 1)
-                add(buf.at[d, x_dn, 1], halves.at[d, 1])
-                send(buf.at[d, x_dn], full.at[d, 1], sx + 4 * d + 3, rx + 4 * d + 3, to_x_dn)
+                arrive(halves.at[k, 0], rx + 4 * k)
+                add(buf.at[d, x_up, 0], halves.at[k, 0])
+                send(buf.at[d, x_up], full.at[k, 0], sx + 4 * k + 2, rx + 4 * k + 2, to_x_up)
+                arrive(halves.at[k, 1], rx + 4 * k + 1)
+                add(buf.at[d, x_dn, 1], halves.at[k, 1])
+                send(buf.at[d, x_dn], full.at[k, 1], sx + 4 * k + 3, rx + 4 * k + 3, to_x_dn)
                 yield
             if k >= lag:
-                along(order[k - lag])
-                yield
-
-        def more(source, r):
-            arrive(source.at[z], r + z)
-            acc[z] = acc[z] + source[z].astype(F32)
-
-        when(z > 0, lambda: more(zu, ru))
-        when(z < ZL - 1, lambda: more(zd, rd))
+                along(k - lag)
+                yield
+            if k - lag == min(H + 1, ZL - 1):
+                gathered(za, ra, other)
+                zt[...] = other[...].astype(BF16)
+                send(zt, zc, sc, rc, at_col(there + i, x))
+                yield
+        gathered(zb, rb_, acc)
+        arrive(zc, rc)
+        acc[...] = acc[...] + zc[...].astype(F32)
         yield
 
-    def broadcast_partner():
-        owner = col // 2
-        core0, y0, zh0 = owner % CORE, (owner // CORE) % Y, owner // (CORE * Y)
-        away = (y + Y - y0) % Y
-        same_core, same_zh = core == core0, zh == zh0
-        chunks = 4
-        size = C // chunks
-        sz, rz = sems("send", chunks), sems("recv", chunks)
-        sy, ry = sems("send", 4 * chunks), sems("recv", 4 * chunks)
-        sc, rc = sems("send", chunks), sems("recv", chunks)
-
-        for parity in range(2):
-            @pl.when(both(row == owner, col % 2 == parity))
+    def exchange():
+        sx, rx = sems("send", 2), sems("recv", 2)
+        own_place = part.at[core, zh, y]
+        for e in range(2):
+            send(gb.at[col, pl.ds(e * cols, cols)], part.at[mirror_core, mirror_y_zh[1], mirror_y_zh[0], col % 2],
+                 sx + e, rx + col % 2, mirror[e], jnp.logical_not(itself[e]))
+
+            @pl.when(itself[e])
             def _():
-                part[...] = gm[:, parity * cols:(parity + 1) * cols, :]
+                part[core, zh, y, e] = gb[col, e * cols:(e + 1) * cols, :]
 
         yield
-        source = both(same_core, away == 0)
-        for n in range(chunks):
-            piece = part.at[pl.ds(n * size, size)]
-            if ZH > 1:
-                send(piece, piece, sz + n, rz + n, to_zh, both(source, same_zh))
-        for n in range(chunks):
-            first = part.at[pl.ds(n * size, size // 2)]
-            second = part.at[pl.ds(n * size + size // 2, size // 2)]
-            piece = part.at[pl.ds(n * size, size)]
-            if ZH > 1:
-                arrive(piece, rz + n, both(source, jnp.logical_not(same_zh)))
-            if Y > 1:
-                send(piece, piece, sy + 4 * n, ry + 4 * n, to_y_up, source)
-                send(piece, piece, sy + 4 * n + 1, ry + 4 * n + 1, to_y_dn, source)
-                yield
-                one, three = both(same_core, away == 1), both(same_core, away == 3)
-                arrive(piece, ry + 4 * n, one)
-                send(first, first, sy + 4 * n + 2, ry + 4 * n + 2, to_y_up, one)
-                arrive(piece, ry + 4 * n + 1, three)
-                send(second, second, sy + 4 * n + 3, ry + 4 * n + 3, to_y_dn, three)
-                yield
-                two = both(same_core, away == 2)
-                arrive(first, ry + 4 * n + 2, two)
-                arrive(second, ry + 4 * n + 3, two)
-            if CORE > 1:
-                send(piece, piece, sc + n, rc + n, to_core, same_core)
-            yield
-        if CORE > 1:
-            for n in range(chunks):
-                piece = part.at[pl.ds(n * size, size)]
-                arrive(piece, rc + n, jnp.logical_not(same_core))
-            yield
+        for e in range(2):
+            arrive(own_place.at[e], rx + e, jnp.logical_not(itself[e]))
 
     def place(p):
         return p % CORE, p // (CORE * Y), (p // CORE) % Y
@@ -349,10 +324,8 @@
         pad = jnp.zeros((LANES - cols, block.shape[1]), block.dtype)
         return jnp.concatenate([block[:cols], pad, block[cols:], pad], axis=0)
 
-    def pair(buf, p, top=0):
-        return jnp.concatenate(
-            [buf[2 * p, top:top + rows], buf[2 * p + 1, top:top + rows]], axis=1
-        )
+    def pair(buf, p):
+        return jnp.concatenate([buf[2 * p], buf[2 * p + 1]], axis=1)
 
     def left_terms(side, buf, target):
         turned = side.astype(F32).T.astype(BF16)
@@ -362,69 +335,128 @@
             target[c, h, j, 0] = term[:, :LANES]
             target[c, h, j, 1] = term[:, LANES:]
 
-    def turned_block(acc, h):
+    def turned_block(acc):
         turn[0:cols, :] = acc
         return turn[...].T[:cols, :cols]
 
-    g = g_ref[...]
-    moment = beta_moment * m_ref[...] + (1.0 - beta_moment) * g.astype(F32)
-    mo_ref[...] = moment
-    gm[col] = jnp.zeros(gm.shape[1:], BF16)
-    lb[col] = jnp.zeros(lb.shape[1:], BF16)
-    rb[core, zh, y] = jnp.zeros(rb.shape[3:], BF16)
-    gm[col, 0:rows, 0:cols] = g
-    gm[col, rows:2 * rows, 0:cols] = moment.astype(BF16)
-    lb[col, :, 0:cols] = l_ref[...]
-    rb[core, zh, y, :, 0:cols] = r_ref[...]
-    turn[...] = jnp.zeros(turn.shape, F32)
+    loads = [
+        pltpu.make_async_copy(source, target, lsem.at[n])
+        for n, (source, target) in enumerate((
+            (g_hbm, g_ref), (m_hbm, m_ref), (r_hbm, r_ref), (l_hbm, l_ref),
+            (sec_hbm, sec_ref), (lf_hbm, lf_ref), (rf_hbm, rf_ref),
+        ))
+    ]
+    for load in loads:
+        load.start()
 
     barrier = pltpu.get_barrier_semaphore()
 
     def greet(device):
         pl.semaphore_signal(barrier, inc=1, device_id=device, device_id_type=MESH)
 
-    always = 0
+    greeted = 0
     for present, devices in (
         (ZH > 1, (to_zh,)), (CORE > 1, (to_core,)), (Y > 1, (to_y_up, to_y_dn)), (X > 1, (to_x_up, to_x_dn)),
+        (True, (at_col(there + i, x),)),
     ):
         if present:
             for device in devices:
                 greet(device)
-                always += 1
-    if ZL > 1:
-        pl.when(z < ZL - 1)(lambda: greet(to_z_up))
-        pl.when(z > 0)(lambda: greet(to_z_dn))
-        inner = both(z > 0, z < ZL - 1)
-        pl.when(inner)(lambda: pl.semaphore_wait(barrier, always + 2))
-        pl.when(jnp.logical_not(inner))(lambda: pl.semaphore_wait(barrier, always + 1))
-    else:
-        pl.semaphore_wait(barrier, always)
-
-    run(gather_cols(gm), gather_rows(rb))
-    rotated = jnp.zeros((2 * rows, LANES), F32)
-    for p in range(R):
-        both_blocks = jnp.concatenate([gm[2 * p], gm[2 * p + 1]], axis=1)
-        rotated = rotated + jnp.dot(both_blocks, spread(rb[place(p)]), preferred_element_type=F32)
-    hb[core, zh, y, :, 0:LANES] = rotated[:rows].astype(BF16)
-    hb[core, zh, y, :, LANES:2 * LANES] = rotated[rows:].astype(BF16)
-
-    def right_factor_terms():
-        left_terms(gm[col, 0:rows, :], gm, gt)
-        yield
-
-    run(gather_rows(hb), gather_cols(lb), right_factor_terms())
+                greeted += 1
+    for j in range(H):
+        pl.when(i != j)(functools.partial(greet, at_col(ours + j, x)))
+    greeted += H - 1
+    edge = jnp.logical_or(z == H - 1, z == H)
+    if H > 1:
+        pl.when(z == H - 1)(lambda: greet(to_z_up))
+        pl.when(z == H)(lambda: greet(to_z_dn))
+
+    for e in range(2):
+        pl.when(jnp.logical_not(itself[e]))(functools.partial(greet, mirror[e]))
+    expected = greeted + jnp.where(row == col // 2, 1, 2)
+    if H > 1:
+        expected = expected + jnp.where(edge, 1, 0)
+
+    gb[col] = jnp.zeros(gb.shape[1:], BF16)
+    mb[col] = jnp.zeros(mb.shape[1:], BF16)
+    lb[col] = jnp.zeros(lb.shape[1:], BF16)
+    rb[core, zh, y] = jnp.zeros(rb.shape[3:], BF16)
+    facing[...] = jnp.zeros(facing.shape, BF16)
+    turn[...] = jnp.zeros(turn.shape, F32)
+    for load in loads[:4]:
+        load.wait()
+    g = g_ref[...]
+    moment = beta_moment * m_ref[...] + (1.0 - beta_moment) * g.astype(F32)
+    mo_ref[...] = moment
+    gb[col, :, 0:cols] = g
+    mb[col, :, 0:cols] = moment.astype(BF16)
+    lb[col, :, 0:cols] = l_ref[...]
+    rb[core, zh, y, :, 0:cols] = r_ref[...]
+
+    pl.semaphore_wait(barrier, expected)
+
+    def rotate(source, target):
+        rotated = jnp.zeros((rows, LANES), F32)
+        for p in range(R):
+            rotated = rotated + jnp.dot(pair(source, p), spread(rb[place(p)]), preferred_element_type=F32)
+        target[core, zh, y] = rotated.astype(BF16)
+
+    ready = []
+
+    def gradient_steps():
+        yield from gather_cols(gb)
+        while not ready:
+            yield
+        rotate(gb, hg)
+        yield from gather_rows(hg)
+
+    factor = scatter_rows(gt, gt_core, gt_half, gt_full, gt_zs, gt_zr, gt_acc)
+
+    def moment_steps():
+        for _ in range(MOMENT_LATER):
+            yield
+        yield from gather_cols(mb)
+        rotate(mb, hm)
+        rest = gather_rows(hm)
+        next(rest)
+        left_terms(gb[col], gb, gt)
+        next(factor)
+        yield from rest
+
+    def basis_steps():
+        for _ in range(BASIS_LATER):
+            yield
+        yield from gather_cols(lb)
+
+    def other_steps():
+        swap = exchange()
+        next(swap)
+        yield from gather_rows(rb)
+        ready.append(True)
+        yield from swap
+        yield from gather_rows(part)
+
+    run(gradient_steps(), moment_steps(), basis_steps(), other_steps())
+    for load in loads[4:]:
+        load.wait()
     rot = jnp.zeros((rows, 2 * LANES), F32)
     for p in range(R):
-        rot = rot + jnp.dot(pair(lb, p), spread(hb[place(p)]), preferred_element_type=F32)
+        both_rotated = jnp.concatenate([spread(hg[place(p)]), spread(hm[place(p)])], axis=1)
+        rot = rot + jnp.dot(pair(lb, p), both_rotated, preferred_element_type=F32)
     grad_rot, moment_rot = rot[:, 0:cols], rot[:, LANES:LANES + cols]
     second = beta_second * sec_ref[...] + (1.0 - beta_second) * grad_rot * grad_rot
     so_ref[...] = second
     direction = moment_rot / (jnp.sqrt(second) + epsilon)
-    facing[...] = jnp.zeros(facing.shape, BF16)
     facing[:, 0:cols] = direction.astype(BF16)
 
     left_terms(facing[...], lb, bt)
-    run(scatter_rows(bt, bt_core, bt_half, bt_full, bt_zs, bt_zr, bt_acc))
+    main = scatter_rows(bt, bt_core, bt_half, bt_full, bt_zs, bt_zr, bt_acc)
+    next(main)
+    next(factor)
+    next(factor)
+    run(main)
+    next(factor, None)
+    next(factor, None)
     back = jnp.concatenate([bt_acc[0], bt_acc[1]], axis=1).astype(BF16)
     back = jnp.concatenate([back, jnp.zeros((LANES - cols, 2 * LANES), BF16)], axis=0)
 
@@ -434,22 +466,25 @@
             c = 2 * p + k
             for h in range(2):
                 ut[c // X, c % X, h] = term[k * cols:(k + 1) * cols, h * LANES:(h + 1) * LANES]
-    run(
-        scatter_cols(ut, ut_half, ut_full, ut_zs, ut_zu, ut_zd, ut_acc),
-        scatter_rows(gt, gt_core, gt_half, gt_full, gt_zs, gt_zr, gt_acc),
-        broadcast_partner(),
-    )
+    main = scatter_cols(ut, ut_half, ut_full, ut_zs, ut_za, ut_zb, ut_zt, ut_zc, ut_other, ut_acc)
+    for k in range(8):
+        next(main, None)
+        if k % 2 == 1:
+            next(factor, None)
+    run(factor)
     left = jnp.zeros((rows, cols), F32)
     for p in range(R):
         left = left + lax.dot_general(
-            pair(gm, p), jnp.concatenate([part[2 * p], part[2 * p + 1]], axis=1),
+            pair(gb, p), jnp.concatenate([part[place(p)][0], part[place(p)][1]], axis=1),
             (((1,), (1,)), ((), ())), preferred_element_type=F32,
         )
     lo_ref[...] = beta_factor * lf_ref[...] + (1.0 - beta_factor) * left
     for h in range(2):
-        part_rows = pl.ds(h * cols, cols)
-        ro_ref[part_rows, :] = beta_factor * rf_ref[part_rows, :] + (1.0 - beta_factor) * turned_block(gt_acc[h], h)
-        up_ref[part_rows, :] = turned_block(ut_acc[z, h], h).astype(BF16)
+        half_rows = pl.ds(h * cols, cols)
+        ro_ref[half_rows, :] = beta_factor * rf_ref[half_rows, :] + (1.0 - beta_factor) * turned_block(gt_acc[h])
+    run(main)
+    for h in range(2):
+        up_ref[pl.ds(h * cols, cols), :] = turned_block(ut_acc[h]).astype(BF16)
 
     for condition, copy in pending:
         when(condition, copy.wait_send)
@@ -473,22 +508,23 @@
     return pl.pallas_call(
         functools.partial(kernel, dims),
         out_shape=(block, block, block, block, jax.ShapeDtypeStruct((rows, cols), BF16)),
-        in_specs=[pl.BlockSpec(memory_space=pltpu.VMEM)] * 7,
+        in_specs=[pl.BlockSpec(memory_space=pl.ANY)] * 7,
         out_specs=[pl.BlockSpec(memory_space=pltpu.VMEM)] * 5,
         scratch_shapes=[
-            pltpu.VMEM((C, 2 * rows, LANES), BF16),
-            pltpu.VMEM((C, rows, LANES), BF16),
-            pltpu.VMEM((CORE, ZH, Y, rows, LANES), BF16),
-            pltpu.VMEM((CORE, ZH, Y, rows, 2 * LANES), BF16),
+            *(pltpu.VMEM((rows, cols), dtype) for dtype in (BF16, F32, F32, F32, F32, BF16, BF16)),
+            *(pltpu.VMEM((C, rows, LANES), BF16) for _ in range(3)),
+            *(pltpu.VMEM((CORE, ZH, Y, rows, LANES), BF16) for _ in range(3)),
             *row_sum(),
             *row_sum(),
             half_blocks(ZL, X), pltpu.VMEM((ZL, 2, cols, LANES), BF16), half_blocks(ZL, 2),
-            half_blocks(ZL), half_blocks(ZL), half_blocks(ZL), half_blocks(ZL, dtype=F32),
-            pltpu.VMEM((C, cols, LANES), BF16),
+            half_blocks(ZL), half_blocks(ZL // 2), half_blocks(ZL // 2), half_blocks(), half_blocks(),
+            half_blocks(dtype=F32), half_blocks(dtype=F32),
+            half_blocks(CORE, ZH, Y),
             pltpu.VMEM((LANES, LANES), F32),
             pltpu.VMEM((rows, LANES), BF16),
-            pltpu.SemaphoreType.DMA((256,)),
-            pltpu.SemaphoreType.DMA((256,)),
+            pltpu.SemaphoreType.DMA((320,)),
+            pltpu.SemaphoreType.DMA((320,)),
+            pltpu.SemaphoreType.DMA((7,)),
         ],
         compiler_params=pltpu.CompilerParams(
             collective_id=0, has_side_effects=True, vmem_limit_bytes=48 << 20

time: 225 us -> 153 us (0.68)
  the two profiles are of different devices: /device:TPU:384 before, /device:TPU:32 now
where the time goes in v2:
time: 153 us
  Pallas kernels  143 us (93%)
  local copies, waits for them, and re-layouts  9.25 us (6%)
    pallas_call x1, Pallas kernels, per_device(): pl.pallas_call(functools.partial(kernel, dims), out_shape=(block, block,...  143 us
    unnamed x19, local copies, waits for them, and re-layouts  9.25 us

profile of v2, /device:TPU:32, one launch (start us, length us, event | category | flops | bytes accessed | tf_op | source)
XLA Modules:
  0.0 153.1 jit_solution(5814476835839997525)
XLA Ops:
  0.6 0.0 copy-start
  0.6 0.9 copy-done
  1.5 0.0 copy-start.1
  1.5 0.9 copy-done.1
  2.4 0.0 copy-start.2
  2.4 0.9 copy-done.2
  3.3 0.0 copy-start.3
  3.3 0.9 copy-done.3
  4.2 0.0 copy-start.4
  4.2 0.8 copy-done.4
  5.0 0.0 copy-start.5
  5.1 0.8 copy-done.5
  5.9 0.0 copy-start.6
  5.9 0.8 copy-done.6
  6.7 143.1 %shard_map.110 = (f32[224,112]{1,0:T(8,128)S(1)}, f32[224,112]{1,0:T(8,128)S(1)}, f32[224,112]{1,0:T(8,128)S(1)}, f32[224,112]{1,0:T(8,128)S(1)}, bf16[224,112]{1,0:T(8,128)(2,1)S(1)}) custom-call(bf16[224,112]{1,0:T(8,128)(2,1)S(1)} %copy-done.4, f32[224,112]{1,0:T(8,128)S(1)} %copy-done, f32[224,112]{1,0:T(8,128)S(1)} %copy-done.1, ...), custom_call_target="tpu_custom_call" | custom-call | tf_op jit(solution)/shard_map/pallas_call | solution.py:508
  149.8 0.6 copy.17
  150.5 0.6 copy.18
  151.1 0.6 copy.19
  151.8 0.6 copy.20
  152.4 0.6 copy.21
Async XLA Ops:
  0.6 0.9 copy-start
  1.5 0.9 copy-start.1
  2.4 0.9 copy-start.2
  3.3 0.9 copy-start.3
  4.2 0.8 copy-start.4
  5.0 0.8 copy-start.5
  5.9 0.8 copy-start.6

commit v3 on v2

--- a/solution.py
+++ b/solution.py
@@ -17,9 +17,12 @@
 BF16 = jnp.bfloat16
 F32 = jnp.float32
 DIMS = (2, 4, 2, 8, 4)
-LAG = 1
-MOMENT_LATER = 0
-BASIS_LATER = 0
+LAG = 2
+LEFT_FROM = 0
+LEFT_EVERY = 2
+FACTOR_AT = {0: 1, 4: 1, 10: 1}
+PARTNER_AT = {0: 2, 4: 1, 5: 1, 8: 1, 9: 1, 12: 1}
+RIGHT_AT = {3: 1, 9: 2, 11: 1, 12: 1, 13: 2}
 
 
 def run(*steps):
@@ -110,6 +113,7 @@
     def gather_cols(buf):
         half = buf.shape[1] // 2
         low, high = pl.ds(0, half), pl.ds(half, half)
+        lag = min(LAG, ZL)
         sz, rz = sems("send", 2 * ZL), sems("recv", ZL)
         sx, rx = sems("send", 4 * ZL), sems("recv", 4 * ZL)
 
@@ -145,10 +149,10 @@
                     send(here, here, sx + 4 * zo, rx + 4 * zo, to_x_up, ok)
                     send(here, here, sx + 4 * zo + 1, rx + 4 * zo + 1, to_x_dn, ok)
             yield
-            if t >= LAG:
-                turn_corner(t - LAG)
-                yield
-        for t in range(ZL - LAG, ZL):
+            if t >= lag:
+                turn_corner(t - lag)
+                yield
+        for t in range(ZL - lag, ZL):
             turn_corner(t)
             yield
         if X > 1:
@@ -156,6 +160,45 @@
                 arrive(buf.at[slot(zo, x_far), low], rx + 4 * zo + 2)
                 arrive(buf.at[slot(zo, x_far), high], rx + 4 * zo + 3)
             yield
+
+    def gather_z(buf):
+        sz, rz = sems("send", 2 * ZL), sems("recv", ZL)
+        for t in range(ZL):
+            ways = [(z, None, 0)] if t == 0 else [(z - t, z >= t, 1), (z + t, z + t < ZL, -1)]
+            for zo, ok, way in ways:
+                here = buf.at[zo * X + x]
+                if t > 0:
+                    arrive(here, rz + zo, ok)
+                if way >= 0 and t < ZL - 1:
+                    send(here, here, sz + zo, rz + zo, to_z_up, both(ok, z < ZL - 1))
+                if way <= 0 and t < ZL - 1:
+                    send(here, here, sz + ZL + zo, rz + zo, to_z_dn, both(ok, z > 0))
+            yield
+
+    def gather_x(buf):
+        if X == 1:
+            return
+        half = buf.shape[1] // 2
+        low, high = pl.ds(0, half), pl.ds(half, half)
+        sx, rx = sems("send", 4 * ZL), sems("recv", 4 * ZL)
+        for zo in range(ZL):
+            here = buf.at[zo * X + x]
+            send(here, here, sx + 4 * zo, rx + 4 * zo, to_x_up)
+            send(here, here, sx + 4 * zo + 1, rx + 4 * zo + 1, to_x_dn)
+        yield
+        for zo in range(ZL):
+            below, above = buf.at[zo * X + x_dn], buf.at[zo * X + x_up]
+            arrive(below, rx + 4 * zo)
+            send(below.at[low], below.at[low], sx + 4 * zo + 2, rx + 4 * zo + 2, to_x_up)
+            arrive(above, rx + 4 * zo + 1)
+            send(above.at[high], above.at[high], sx + 4 * zo + 3, rx + 4 * zo + 3, to_x_dn)
+            if zo % 2 == 1:
+                yield
+        for zo in range(ZL):
+            far = buf.at[zo * X + x_far]
+            arrive(far.at[low], rx + 4 * zo + 2)
+            arrive(far.at[high], rx + 4 * zo + 3)
+        yield
 
     def gather_rows(buf):
         half = buf.shape[3] // 2
@@ -401,42 +444,31 @@
             rotated = rotated + jnp.dot(pair(source, p), spread(rb[place(p)]), preferred_element_type=F32)
         target[core, zh, y] = rotated.astype(BF16)
 
-    ready = []
-
-    def gradient_steps():
-        yield from gather_cols(gb)
-        while not ready:
-            yield
-        rotate(gb, hg)
-        yield from gather_rows(hg)
-
     factor = scatter_rows(gt, gt_core, gt_half, gt_full, gt_zs, gt_zr, gt_acc)
-
-    def moment_steps():
-        for _ in range(MOMENT_LATER):
-            yield
-        yield from gather_cols(mb)
-        rotate(mb, hm)
-        rest = gather_rows(hm)
-        next(rest)
-        left_terms(gb[col], gb, gt)
-        next(factor)
-        yield from rest
-
-    def basis_steps():
-        for _ in range(BASIS_LATER):
-            yield
-        yield from gather_cols(lb)
-
-    def other_steps():
-        swap = exchange()
-        next(swap)
-        yield from gather_rows(rb)
-        ready.append(True)
-        yield from swap
-        yield from gather_rows(part)
-
-    run(gradient_steps(), moment_steps(), basis_steps(), other_steps())
+    swap, partner = exchange(), gather_rows(part)
+    left_z, left_x = gather_z(lb), gather_x(lb)
+    grad_cols, moment_cols, right_rows = gather_cols(gb), gather_cols(mb), gather_rows(rb)
+    for k in range(14):
+        next(grad_cols, None)
+        next(moment_cols, None)
+        for _ in range(RIGHT_AT.get(k, 0)):
+            next(right_rows, None)
+        if k >= LEFT_FROM and (k - LEFT_FROM) % LEFT_EVERY == 0:
+            next(left_z, None)
+    run(grad_cols, moment_cols, right_rows)
+    rotate(gb, hg)
+    grad_rows, moment_rows = gather_rows(hg), gather_rows(hm)
+    next(grad_rows)
+    rotate(mb, hm)
+    next(moment_rows)
+    run(left_z)
+    next(left_x, None)
+    next(swap)
+    left_terms(gb[col], gb, gt)
+    next(factor)
+    run(grad_rows, moment_rows, left_x)
+    next(factor)
+    next(factor)
     for load in loads[4:]:
         load.wait()
     rot = jnp.zeros((rows, 2 * LANES), F32)
@@ -452,8 +484,8 @@
     left_terms(facing[...], lb, bt)
     main = scatter_rows(bt, bt_core, bt_half, bt_full, bt_zs, bt_zr, bt_acc)
     next(main)
-    next(factor)
-    next(factor)
+    run(swap)
+    next(partner)
     run(main)
     next(factor, None)
     next(factor, None)
@@ -467,11 +499,13 @@
             for h in range(2):
                 ut[c // X, c % X, h] = term[k * cols:(k + 1) * cols, h * LANES:(h + 1) * LANES]
     main = scatter_cols(ut, ut_half, ut_full, ut_zs, ut_za, ut_zb, ut_zt, ut_zc, ut_other, ut_acc)
-    for k in range(8):
+    for k in range(14):
         next(main, None)
-        if k % 2 == 1:
+        for _ in range(FACTOR_AT.get(k, 0)):
             next(factor, None)
-    run(factor)
+        for _ in range(PARTNER_AT.get(k, 0)):
+            next(partner, None)
+    run(factor, partner)
     left = jnp.zeros((rows, cols), F32)
     for p in range(R):
         left = left + lax.dot_general(
@@ -527,7 +561,7 @@
             pltpu.SemaphoreType.DMA((7,)),
         ],
         compiler_params=pltpu.CompilerParams(
-            collective_id=0, has_side_effects=True, vmem_limit_bytes=48 << 20
+            collective_id=0, has_side_effects=True, vmem_limit_bytes=60 << 20
         ),
     )(gradient, moment, second, left_factor, right_factor, left_basis_t, right_basis)
 

time: 153 us -> 133 us (0.87)
  the two profiles are of different devices: /device:TPU:32 before, /device:TPU:96 now
where the time goes in v3:
time: 133 us
  Pallas kernels  127 us (95%)
  local copies, waits for them, and re-layouts  4.93 us (4%)
    pallas_call x1, Pallas kernels, per_device(): pl.pallas_call(functools.partial(kernel, dims), out_shape=(block, block,...  127 us
    unnamed x13, local copies, waits for them, and re-layouts  4.93 us

profile of v3, /device:TPU:96, one launch (start us, length us, event | category | flops | bytes accessed | tf_op | source)
XLA Modules:
  0.0 132.6 jit_solution(11716948527116479345)
XLA Ops:
  0.6 127.0 %shard_map.110 = (f32[224,112]{1,0:T(8,128)}, f32[224,112]{1,0:T(8,128)}, f32[224,112]{1,0:T(8,128)}, f32[224,112]{1,0:T(8,128)}, bf16[224,112]{1,0:T(8,128)(2,1)}) custom-call(bf16[224,112]{1,0:T(8,128)(2,1)} %g_hbm.1, f32[224,112]{1,0:T(8,128)} %m_hbm.1, f32[224,112]{1,0:T(8,128)} %sec_hbm.1, f32[224,112]{1,0:T(8,128)} %lf_hbm.1, f32[224,112]{1,0:T(8,128)} %rf_hbm.1, ...), custom_call_target="tpu_custom_call" | custom-call | tf_op jit(solution)/shard_map/pallas_call | solution.py:542
  127.6 0.0 copy-start.2
  127.6 1.6 %copy.17 = f32[224,112]{1,0:T(8,128)} copy(f32[224,112]{1,0:T(8,128)} %get-tuple-element.10) | data formatting | bytes 200704
  129.2 0.0 copy-done.2
  129.2 0.0 copy-start.1
  129.2 0.6 copy.18
  129.9 0.3 copy-done.1
  130.2 0.0 copy-start
  130.2 0.6 copy.19
  130.8 0.3 copy-done
  131.1 0.0 copy-start.3
  131.1 0.6 copy.20
  131.7 0.2 copy-done.3
  131.9 0.6 copy.21
Async XLA Ops:
  127.6 1.6 %copy-start.2 = (f32[224,112]{1,0:T(8,128)S(1)}, f32[224,112]{1,0:T(8,128)}, u32[]{:S(2)}) copy-start(f32[224,112]{1,0:T(8,128)} %get-tuple-element.11) | copy-start | bytes 301060
  129.2 0.9 copy-start.1
  130.2 0.9 copy-start
  131.1 0.8 copy-start.3

commit v4 on v3

--- a/solution.py
+++ b/solution.py
@@ -499,7 +499,7 @@
             for h in range(2):
                 ut[c // X, c % X, h] = term[k * cols:(k + 1) * cols, h * LANES:(h + 1) * LANES]
     main = scatter_cols(ut, ut_half, ut_full, ut_zs, ut_za, ut_zb, ut_zt, ut_zc, ut_other, ut_acc)
-    for k in range(14):
+    for k in range(18):
         next(main, None)
         for _ in range(FACTOR_AT.get(k, 0)):
             next(factor, None)

time: 133 us -> 134 us (level)
  the two profiles are of different devices: /device:TPU:96 before, /device:TPU:64 now
where the time goes in v4:
time: 134 us
  Pallas kernels  128 us (96%)
  local copies, waits for them, and re-layouts  4.93 us (4%)
    pallas_call x1, Pallas kernels, per_device(): pl.pallas_call(functools.partial(kernel, dims), out_shape=(block, block,...  128 us
    unnamed x13, local copies, waits for them, and re-layouts  4.93 us

profile of v4, /device:TPU:64, one launch (start us, length us, event | category | flops | bytes accessed | tf_op | source)
XLA Modules:
  0.0 133.6 jit_solution(34475161348000578)
XLA Ops:
  0.6 128.0 %shard_map.110 = (f32[224,112]{1,0:T(8,128)}, f32[224,112]{1,0:T(8,128)}, f32[224,112]{1,0:T(8,128)}, f32[224,112]{1,0:T(8,128)}, bf16[224,112]{1,0:T(8,128)(2,1)}) custom-call(bf16[224,112]{1,0:T(8,128)(2,1)} %g_hbm.1, f32[224,112]{1,0:T(8,128)} %m_hbm.1, f32[224,112]{1,0:T(8,128)} %sec_hbm.1, f32[224,112]{1,0:T(8,128)} %lf_hbm.1, f32[224,112]{1,0:T(8,128)} %rf_hbm.1, ...), custom_call_target="tpu_custom_call" | custom-call | tf_op jit(solution)/shard_map/pallas_call | solution.py:542
  128.6 0.0 copy-start.2
  128.6 1.6 %copy.17 = f32[224,112]{1,0:T(8,128)} copy(f32[224,112]{1,0:T(8,128)} %get-tuple-element.10) | data formatting | bytes 200704
  130.2 0.0 copy-done.2
  130.2 0.0 copy-start.1
  130.2 0.6 copy.18
  130.9 0.3 copy-done.1
  131.2 0.0 copy-start
  131.2 0.6 copy.19
  131.8 0.3 copy-done
  132.1 0.0 copy-start.3
  132.1 0.6 copy.20
  132.8 0.2 copy-done.3
  133.0 0.6 copy.21
Async XLA Ops:
  128.6 1.6 %copy-start.2 = (f32[224,112]{1,0:T(8,128)S(1)}, f32[224,112]{1,0:T(8,128)}, u32[]{:S(2)}) copy-start(f32[224,112]{1,0:T(8,128)} %get-tuple-element.11) | copy-start | bytes 301060
  130.2 0.9 copy-start.1
  131.2 0.9 copy-start
  132.1 0.8 copy-start.3
